TPU v7x, 32 devices: a whole 2x2x4 slice. The times are simulated.
32 devices in a mesh: row: 8 (over y, x, core), col: 4 (over z).
Axes of the slice: x: 2, y: 2, z: 4, core: 2. Of those that a mesh axis runs over, the one named last changes fastest.
Arguments:
- row_frames: float32 [3, 1024, 256], P(None, ('row', 'col')), may hold values from -40 to 40, as said below
- col_frames: float32 [3, 1024, 256], P(None, ('col', 'row')), may hold values from -40 to 40, as said below
- vectors: float32 [64, 1024], P(None, ('col', 'row')), may hold values from -6 to 6
Outputs:
- embedding_product: float32 [64, 1024], P(None, ('row', 'col'))
Inputs may be any that keep to these rules, and one draw needn't show every extreme that they name: `row_frames`: frames of one chain of 256 atoms, each rigidly rotated and moved and perturbed by its own amount. `col_frames`: frames of one chain of 256 atoms, each rigidly rotated and moved and perturbed by its own amount.
All inputs are finite; a program needn't handle non-finite values.
Results may differ from a plain program's by a relative error of at most 0.00017.
Values sent between devices are 32-bit elements; how exact they have to be, the bound alone decides.
No kernel may reach another device: no remote copies, remote signals or barrier semaphores. Data moves between devices by JAX's collectives and lax.ppermute only.
A program may use at most 64 MiB of HBM per device.

v0:
```python
import functools

import jax
import jax.numpy as jnp
from jax import lax
from jax.experimental import pallas as pl
from jax.experimental.pallas import tpu as pltpu
from jax.sharding import PartitionSpec as P

NEWTON = 8
BAND = 2.0
LANES = 128
VM = pl.BlockSpec(memory_space=pltpu.VMEM)
NT = (((1,), (1,)), ((), ()))


def centre(frames):
    return frames - jnp.mean(frames, axis=-1, keepdims=True)


def split(x):
    high = x.astype(jnp.bfloat16)
    low = (x - high.astype(jnp.float32)).astype(jnp.bfloat16)
    return high, low


def copy_kernel(in_ref, out_ref):
    out_ref[...] = in_ref[...]


def pack_kernel(frames, nv, in_ref, out_ref):
    used = in_ref.shape[0] - frames
    groups = in_ref.shape[1] // nv
    step = frames // groups
    out_ref[0:used, :] = in_ref[0:used, :]
    out_ref[used:, :] = jnp.concatenate(
        [in_ref[used + group * step:used + (group + 1) * step, 0:nv] for group in range(groups)], axis=1
    )


def copy_kernel(in_ref, out_ref):
    out_ref[...] = in_ref[...]


def columns_kernel(n_blocks, *refs):
    for at in range(n_blocks):
        refs[-1][at] = refs[at][...]


def inverse(x):
    guess = pl.reciprocal(x, approx=True)
    return guess * (2.0 - x * guess)


def eigen_tile(m, half_norm, atoms):
    s00, s01, s02, s10, s11, s12, s20, s21, s22 = m
    coef_two = -2.0 * (
        s00 * s00 + s01 * s01 + s02 * s02 + s10 * s10 + s11 * s11 + s12 * s12 + s20 * s20 + s21 * s21 + s22 * s22
    )
    coef_one = 8.0 * (s00 * s12 * s21 + s11 * s20 * s02 + s22 * s01 * s10) - 8.0 * (
        s00 * s11 * s22 + s12 * s20 * s01 + s21 * s10 * s02
    )
    k00 = s00 + s11 + s22
    k11 = s00 - s11 - s22
    k22 = s11 - s00 - s22
    k33 = s22 - s00 - s11
    k01 = s12 - s21
    k02 = s20 - s02
    k03 = s01 - s10
    k12 = s01 + s10
    k13 = s20 + s02
    k23 = s12 + s21
    top0 = k00 * k11 - k01 * k01
    top1 = k00 * k12 - k01 * k02
    top2 = k00 * k13 - k01 * k03
    top3 = k01 * k12 - k11 * k02
    top4 = k01 * k13 - k11 * k03
    top5 = k02 * k13 - k12 * k03
    low0 = k02 * k13 - k03 * k12
    low1 = k02 * k23 - k03 * k22
    low2 = k02 * k33 - k03 * k23
    low3 = k12 * k23 - k13 * k22
    low4 = k12 * k33 - k13 * k23
    low5 = k22 * k33 - k23 * k23
    coef_zero = top0 * low5 - top1 * low4 + top2 * low3 + top3 * low2 - top4 * low1 + top5 * low0
    eigen = half_norm
    twice = coef_two + coef_two
    for _ in range(NEWTON):
        eigen_sq = eigen * eigen
        value = (eigen_sq + coef_two) * eigen_sq + coef_one * eigen + coef_zero
        slope = (4.0 * eigen_sq + twice) * eigen + coef_one
        eigen = eigen - value * inverse(slope)
    squared = jnp.maximum(2.0 * (half_norm - eigen) / atoms, 0.0)
    return jnp.exp(-squared / BAND)


def column_side(blocks_ref, frames):
    count, _, atoms = blocks_ref.shape
    cols = [
        centre(jnp.concatenate([blocks_ref[at, comp * frames:(comp + 1) * frames, :] for at in range(count)], axis=0))
        for comp in range(3)
    ]
    col_square = cols[0] * cols[0] + cols[1] * cols[1] + cols[2] * cols[2]
    high, low = split(col_square)
    rest = (col_square - high.astype(jnp.float32) - low.astype(jnp.float32)).astype(jnp.bfloat16)
    norm = lax.dot_general(
        jnp.ones((8, 3 * atoms), jnp.bfloat16), jnp.concatenate([high, low, rest], axis=1), NT,
        preferred_element_type=jnp.float32,
    )
    high, low = split(jnp.concatenate(cols, axis=0))
    return jnp.concatenate([high, high, low], axis=1), norm


def vector_side(blocks_ref, frames, nv):
    count, _, atoms = blocks_ref.shape
    groups = atoms // nv
    step = frames // groups
    lane = lax.broadcasted_iota(jnp.int32, (step, LANES), 1)
    parts = []
    for at in range(count):
        for group in range(groups):
            place = group * nv
            piece = blocks_ref[at, 3 * frames:, place // LANES * LANES:place // LANES * LANES + LANES]
            if place % LANES:
                piece = pltpu.roll(piece, LANES - place % LANES, 1)
            parts.append(jnp.where(lane < nv, piece, jnp.where(lane == nv, 1.0, 0.0)))
    high, low = split(jnp.concatenate(parts, axis=0))
    return [high, high, low]


def row_side(slots):
    rows = [centre(jnp.concatenate([ref[comp] for ref in slots], axis=0)) for comp in range(3)]
    square = jnp.sum(rows[0] * rows[0] + rows[1] * rows[1] + rows[2] * rows[2], axis=1, keepdims=True)
    high, low = split(jnp.concatenate(rows, axis=0))
    return jnp.concatenate([high, low, high], axis=1), jnp.broadcast_to(square, (square.shape[0], LANES))


def kernel_tile(rows, row_norm, side, norm, moment, tile):
    count = row_norm.shape[0]
    count_cols = norm.shape[1]
    atoms = side.shape[1] // 3
    moment[0:3 * count, :] = lax.dot_general(rows, side, NT, preferred_element_type=jnp.float32)
    for at in range(0, count, 8):
        m = [
            moment[a * count + at:a * count + at + 8, b * count_cols:(b + 1) * count_cols]
            for a in range(3) for b in range(3)
        ]
        half_norm = 0.5 * (row_norm[at:at + 8, 0:1] + norm[0:1, :])
        tile[at:at + 8, :] = eigen_tile(m, half_norm, atoms)


def early_kernel(n_early, nv, *refs):
    slots, blocks_ref = refs[:n_early], refs[n_early]
    rows_ref, row_norm_ref, tile_ref, side_ref, norm_ref, vec_ref, moment = refs[n_early + 1:]
    frames = slots[0].shape[1]
    groups, count, _ = tile_ref.shape
    side, norm = column_side(blocks_ref, frames)
    side_ref[...] = side
    norm_ref[...] = norm
    vec_ref[...] = jnp.concatenate(vector_side(blocks_ref, frames, nv), axis=0)
    for group in range(groups):
        own = slots[group * count // frames:(group + 1) * count // frames]
        used = len(own) * frames
        rows, row_norm = row_side(own)
        for comp in range(3):
            rows_ref[group, comp * count:comp * count + used, :] = rows[comp * used:(comp + 1) * used]
        row_norm_ref[group, 0:used, :] = row_norm
        kernel_tile(rows, row_norm, side, norm, moment, tile_ref.at[group, 0:used])


def last_kernel(row_ref, side_ref, norm_ref, *refs):
    rows_ref, row_norm_ref, tile_ref, moment = refs[3:]
    frames = row_ref.shape[1]
    groups, count, _ = tile_ref.shape
    rows, row_norm = row_side([row_ref])
    for comp in range(3):
        rows_ref[groups - 1, (comp + 1) * count - frames:(comp + 1) * count, :] = rows[comp * frames:(comp + 1) * frames]
    row_norm_ref[groups - 1, count - frames:, :] = row_norm
    kernel_tile(rows, row_norm, side_ref[...], norm_ref[...], moment, tile_ref.at[groups - 1, count - frames:count])


def second_kernel(frames, nv, rows_ref, row_norm_ref, tile_ref, vec_ref, blocks_ref, *refs):
    out_refs, moment, other_tile = refs[:-2], refs[-2], refs[-1]
    groups, count, _ = tile_ref.shape
    side, norm = column_side(blocks_ref, frames)
    vecs = jnp.concatenate([vec_ref[...]] + vector_side(blocks_ref, frames, nv), axis=0)
    for group in range(groups):
        kernel_tile(rows_ref[group], row_norm_ref[group], side, norm, moment, other_tile)
        high, low = split(tile_ref[group])
        other_high, other_low = split(other_tile[...])
        total = jnp.dot(
            jnp.concatenate([high, low, high, other_high, other_low, other_high], axis=1), vecs,
            preferred_element_type=jnp.float32,
        )
        for at in range(count // frames):
            out_refs[group * count // frames + at][...] = total[at * frames:(at + 1) * frames, :]


def finish_kernel(nv, *refs):
    total = refs[0][...]
    for ref in refs[1:-1]:
        total = total + ref[...]
    refs[-1][...] = total[:, 0:nv] / total[:, nv:nv + 1]


def exchange(x, axis, mask, count):
    return lax.ppermute(x, axis, [(at, at ^ mask) for at in range(count)])


def call(kernel, outs, ins, name, scratch=(), megabytes=8, flops=0, aliases=None):
    out_shape = [jax.ShapeDtypeStruct(*out) for out in outs]
    moved = sum(x.size * 4 for x in ins)
    return pl.pallas_call(
        kernel,
        out_shape=out_shape,
        in_specs=[VM] * len(ins),
        out_specs=[VM] * len(outs),
        scratch_shapes=list(scratch),
        input_output_aliases=aliases or {},
        compiler_params=pltpu.CompilerParams(vmem_limit_bytes=megabytes * 1024 * 1024),
        cost_estimate=pl.CostEstimate(flops=flops, bytes_accessed=moved, transcendentals=0),
        name=name,
    )(*ins)


def per_device(n_row, n_col, row_frames, col_frames, vectors):
    comps, frames, atoms = row_frames.shape
    nv = vectors.shape[0]
    f32, bf16 = jnp.float32, jnp.bfloat16
    row_masks = [n_col >> at for at in range(1, n_col.bit_length())]
    col_masks = [1 << at for at in range(1, n_row.bit_length() - 1)]

    packed_shape = (comps * frames + frames * nv // atoms, atoms)
    both = jnp.concatenate(
        [col_frames.reshape(comps * frames, atoms), jnp.pad(vectors.T, ((0, 0), (0, atoms - nv)))], axis=0
    )
    (packed,) = call(functools.partial(pack_kernel, frames, nv), [(packed_shape, f32)], [both], "pack")
    order = [0]
    rows = {0: row_frames}
    for mask in row_masks:
        for slot in list(order):
            got = exchange(rows[slot], "col", mask, n_col)
            if not slot and mask == row_masks[0]:
                (got,) = call(copy_kernel, [(got.shape, f32)], [got], "far_rows", flops=10 << 30)
            rows[slot ^ mask] = got
            order.append(slot ^ mask)
    col_order = [0]
    for mask in col_masks:
        col_order = col_order + [slot ^ mask for slot in col_order]
    cols = [packed] + [exchange(packed, "row", mask, n_row) for mask in col_order[1:]]
    (blocks,) = call(
        functools.partial(columns_kernel, len(cols)), [((len(cols), *packed_shape), f32)],
        [*cols, rows[row_masks[0]]], "columns", flops=10 << 30,
    )
    other = exchange(blocks, "row", 1, n_row)

    half_cols = n_row // 2 * frames
    count = min(n_col, max(1, LANES // frames)) * frames
    groups = n_col * frames // count
    moment = pltpu.VMEM((3 * count, 3 * half_cols), f32)
    tile = pltpu.VMEM((count, half_cols), f32)
    work = 2 * 3 * n_col * frames * 3 * half_cols * 3 * atoms
    outs = [
        ((groups, 3 * count, 3 * atoms), bf16), ((groups, count, LANES), f32), ((groups, count, half_cols), f32),
    ]
    *kept, side, norm, vec = call(
        functools.partial(early_kernel, n_col - 1, nv),
        outs + [((3 * half_cols, 3 * atoms), bf16), ((8, half_cols), f32), ((3 * half_cols, LANES), bf16)],
        [*[rows[slot] for slot in order[:-1]], blocks], "early_tile", [moment], 32, work,
    )
    kept = call(
        last_kernel, outs, [rows[order[-1]], side, norm, *kept], "last_tile",
        [pltpu.VMEM((3 * frames, 3 * half_cols), f32)], 32, work << 8, {3: 0, 4: 1, 5: 2},
    )
    parts = call(
        functools.partial(second_kernel, frames, nv), [((frames, LANES), f32)] * n_col,
        [*kept, vec, other], "second_tile", [moment, tile], 32, work,
    )
    shares = [parts[0]] + [
        exchange(parts[order.index(mask)], "col", mask, n_col) for mask in range(n_col - 1, 0, -1)
    ]
    (result,) = call(functools.partial(finish_kernel, nv), [((frames, nv), f32)], shares, "sum_divide")
    return result.T


def solution(mesh):
    return jax.shard_map(
        functools.partial(per_device, mesh.shape["row"], mesh.shape["col"]),
        mesh=mesh,
        in_specs=(
            P(None, ("row", "col"), None),
            P(None, ("col", "row"), None),
            P(None, ("col", "row")),
        ),
        out_specs=P(None, ("row", "col")),
        check_vma=False,
    )
```

profile of v0, /device:TPU:0, one launch (start us, length us, event | category | flops | bytes accessed | tf_op | source)
XLA Modules:
  0.0 24.7 jit_solution(4222401828231981512)
XLA Ops:
  0.0 4.0 %collective-permute-start = (f32[3,32,256]{2,1,0:T(8,128)}, f32[3,32,256]{2,1,0:T(8,128)S(1)}, u32[]{:S(2)}, u32[]{:S(2)}) collective-permute-start(f32[3,32,256]{2,1,0:T(8,128)} %refs_0_.1), channel_id=1, source_target_pairs={{0,2},{1,3},{2,0},{3,1},{4,6},{5,7},{6,4},{7,5},{8,10},{9,11},{10,... | collective-permute-start | bytes 294920 | tf_op jit(solution)/shard_map/ppermute | solution.py:207
  4.0 1.6 %collective-permute-start.2 = (f32[3,32,256]{2,1,0:T(8,128)}, f32[3,32,256]{2,1,0:T(8,128)S(1)}, u32[]{:S(2)}, u32[]{:S(2)}) collective-permute-start(f32[3,32,256]{2,1,0:T(8,128)} %refs_0_.1), channel_id=1, source_target_pairs={{0,1},{1,0},{2,3},{3,2},{4,5},{5,4},{6,7},{7,6},{8,9},{9,8},{10,11... | collective-permute-start | bytes 294920 | tf_op jit(solution)/shard_map/ppermute | solution.py:207
  5.6 0.9 %select_maximum_fusion.in_ref = f32[128,256]{1,0:T(8,128)S(1)} fusion(f32[32,64]{1,0:T(8,128)} %bitcast.4, f32[96,256]{1,0:T(8,128)} %bitcast.3), kind=kLoop, calls=%fused_computation | loop fusion | flops 98304 | bytes 237568 | tf_op jit(solution)/shard_map/concatenate | solution.py:234
  6.5 0.1 pack.1.refs_0_
  6.6 2.5 %collective-permute-start.5 = (f32[104,256]{1,0:T(8,128)S(1)}, f32[104,256]{1,0:T(8,128)S(1)}, u32[]{:S(2)}, u32[]{:S(2)}) collective-permute-start(f32[104,256]{1,0:T(8,128)S(1)} %pack.1.refs_0_), channel_id=1, source_target_pairs={{0,24},{4,28},{8,16},{12,20},{16,8},{20,12},{24,0},{28,4},{1,25},{... | collective-permute-start | bytes 319496 | tf_op jit(solution)/shard_map/ppermute | solution.py:207
  9.1 0.5 %collective-permute-start.4 = (f32[104,256]{1,0:T(8,128)S(1)}, f32[104,256]{1,0:T(8,128)S(1)}, u32[]{:S(2)}, u32[]{:S(2)}) collective-permute-start(f32[104,256]{1,0:T(8,128)S(1)} %pack.1.refs_0_), channel_id=1, source_target_pairs={{0,16},{4,20},{8,24},{12,28},{16,0},{20,4},{24,8},{28,12},{1,17},{... | collective-permute-start | bytes 319496 | tf_op jit(solution)/shard_map/ppermute | solution.py:207
  9.6 0.5 %collective-permute-start.3 = (f32[104,256]{1,0:T(8,128)S(1)}, f32[104,256]{1,0:T(8,128)S(1)}, u32[]{:S(2)}, u32[]{:S(2)}) collective-permute-start(f32[104,256]{1,0:T(8,128)S(1)} %pack.1.refs_0_), channel_id=1, source_target_pairs={{0,8},{4,12},{8,0},{12,4},{16,24},{20,28},{24,16},{28,20},{1,9},{5... | collective-permute-start | bytes 319496 | tf_op jit(solution)/shard_map/ppermute | solution.py:207
  10.1 0.0 collective-permute-done.in_ref
  10.1 0.0 copy-start
  10.1 0.5 %collective-permute-start.1 = (f32[3,32,256]{2,1,0:T(8,128)S(1)}, f32[3,32,256]{2,1,0:T(8,128)S(1)}, u32[]{:S(2)}, u32[]{:S(2)}) collective-permute-start(f32[3,32,256]{2,1,0:T(8,128)S(1)} %far_rows.1.refs_4_.refs_1_), channel_id=1, source_target_pairs={{0,1},{1,0},{2,3},{3,2},{4,5},{5,4},{6,7},{7,6},{8,9},{9,8},{10,11... | collective-permute-start | bytes 294920 | tf_op jit(solution)/shard_map/ppermute | solution.py:207
  10.7 2.0 %collective-permute-done.5.refs_3_ = f32[104,256]{1,0:T(8,128)S(1)} collective-permute-done((f32[104,256]{1,0:T(8,128)S(1)}, f32[104,256]{1,0:T(8,128)S(1)}, u32[]{:S(2)}, u32[]{:S(2)}) %collective-permute-start.5) | collective-permute-done | bytes 106528 | tf_op jit(solution)/shard_map/ppermute | solution.py:207
  12.7 1.4 %collective-permute-done.4.refs_2_ = f32[104,256]{1,0:T(8,128)S(1)} collective-permute-done((f32[104,256]{1,0:T(8,128)S(1)}, f32[104,256]{1,0:T(8,128)S(1)}, u32[]{:S(2)}, u32[]{:S(2)}) %collective-permute-start.4) | collective-permute-done | bytes 106528 | tf_op jit(solution)/shard_map/ppermute | solution.py:207
  14.1 0.2 collective-permute-done.3.refs_1_
  14.3 0.1 collective-permute-start.6
  14.4 0.0 collective-permute-done.2.refs_2_
  14.4 0.0 copy-done
  14.4 1.1 %early_tile.1 = (bf16[1,384,768]{2,1,0:T(8,128)(2,1)S(1)}, f32[1,128,128]{2,1,0:T(8,128)S(1)}, f32[1,128,128]{2,1,0:T(8,128)S(1)}, bf16[384,768]{1,0:T(8,128)(2,...) custom-call(f32[3,32,256]{2,1,0:T(8,128)S(1)} %copy-done, f32[3,32,256]{2,1,0:T(8,128)S(1)} %far_rows.1.refs_4_.refs_1_, ...), custom_call_target="tpu_custom_call" | custom-call | flops 226492416 | bytes 720896 | tf_op jit(solution)/shard_map/early_tile/pallas_call | solution.py:213
  15.5 0.0 collective-permute-done.1.row_ref
  15.5 0.5 %last_tile.1 = (bf16[1,384,768]{2,1,0:T(8,128)(2,1)S(1)}, f32[1,128,128]{2,1,0:T(8,128)S(1)}, f32[1,128,128]{2,1,0:T(8,128)S(1)}) custom-call(f32[3,32,256]{2,1,0:T(8,128)S(1)} %collective-permute-done.1.row_ref, bf16[384,768]{1,0:T(8,128)(2,1)S(1)} %get-tuple-element.18.side_ref, ...), custom_call_target="tpu_custom_call", output_to_operand_aliasing={{0}: (3, {}), {1}: (4, {}), {2}: (5, {})} | custom-call | flops 57982058496 | bytes 2592768 | tf_op jit(solution)/shard_map/last_tile/pallas_call | solution.py:213
  16.0 0.1 collective-permute-done.6.blocks_ref
  16.2 1.3 %second_tile.1 = (f32[32,128]{1,0:T(8,128)S(1)}, f32[32,128]{1,0:T(8,128)S(1)}, f32[32,128]{1,0:T(8,128)S(1)}, f32[32,128]{1,0:T(8,128)S(1)}) custom-call(bf16[1,384,768]{2,1,0:T(8,128)(2,1)S(1)} %get-tuple-element.23.rows_ref, f32[1,128,128]{2,1,0:T(8,128)S(1)} %get-tuple-element.24.row_norm_ref, f32[1,128,128]{2,1,0:T(8,128)S(1)} %get-tuple-element.25.tile_ref, ...), custom_call_target="tpu_custom_call" | custom-call | flops 226492416 | bytes 1933312 | tf_op jit(solution)/shard_map/second_tile/pallas_call | solution.py:213
  17.4 1.9 %collective-permute-start.7 = (f32[32,128]{1,0:T(8,128)S(1)}, f32[32,128]{1,0:T(8,128)S(1)}, u32[]{:S(2)}, u32[]{:S(2)}) collective-permute-start(f32[32,128]{1,0:T(8,128)S(1)} %get-tuple-element.28), channel_id=1, source_target_pairs={{0,3},{1,2},{2,1},{3,0},{4,7},{5,6},{6,5},{7,4},{8,11},{9,10},{10,... | collective-permute-start | bytes 49160 | tf_op jit(solution)/shard_map/ppermute | solution.py:207
  19.4 0.1 collective-permute-start.8
  19.4 2.5 %collective-permute-start.9 = (f32[32,128]{1,0:T(8,128)S(1)}, f32[32,128]{1,0:T(8,128)S(1)}, u32[]{:S(2)}, u32[]{:S(2)}) collective-permute-start(f32[32,128]{1,0:T(8,128)S(1)} %get-tuple-element.30), channel_id=1, source_target_pairs={{0,1},{1,0},{2,3},{3,2},{4,5},{5,4},{6,7},{7,6},{8,9},{9,8},{10,11... | collective-permute-start | bytes 49160 | tf_op jit(solution)/shard_map/ppermute | solution.py:207
  21.9 1.3 %collective-permute-done.7.refs_1_ = f32[32,128]{1,0:T(8,128)S(1)} collective-permute-done((f32[32,128]{1,0:T(8,128)S(1)}, f32[32,128]{1,0:T(8,128)S(1)}, u32[]{:S(2)}, u32[]{:S(2)}) %collective-permute-start.7) | collective-permute-done | bytes 16416 | tf_op jit(solution)/shard_map/ppermute | solution.py:207
  23.2 0.8 %collective-permute-done.8.refs_2_ = f32[32,128]{1,0:T(8,128)S(1)} collective-permute-done((f32[32,128]{1,0:T(8,128)S(1)}, f32[32,128]{1,0:T(8,128)S(1)}, u32[]{:S(2)}, u32[]{:S(2)}) %collective-permute-start.8) | collective-permute-done | bytes 16416 | tf_op jit(solution)/shard_map/ppermute | solution.py:207
  24.0 0.0 collective-permute-done.9.refs_3_
  24.0 0.7 %sum_divide.1 = f32[32,64]{1,0:T(8,128)} custom-call(f32[32,128]{1,0:T(8,128)S(1)} %get-tuple-element.27.refs_0_, f32[32,128]{1,0:T(8,128)S(1)} %collective-permute-done.7.refs_1_, f32[32,128]{1,0:T(8,128)S(1)} %collective-permute-done.8.refs_2_, f32[32,128]{1,0:T(8,128)S(1)} %collective-permute-done.9.refs_3_), custom_call_target="tpu_custom_call" | custom-call | bytes 65536 | tf_op jit(solution)/shard_map/sum_divide/pallas_call | solution.py:213
  (2 shorter events, 0.0 us)
Async XLA Ops:
  0.0 10.1 %collective-permute-start = (f32[3,32,256]{2,1,0:T(8,128)}, f32[3,32,256]{2,1,0:T(8,128)S(1)}, u32[]{:S(2)}, u32[]{:S(2)}) collective-permute-start(f32[3,32,256]{2,1,0:T(8,128)} %refs_0_.1), channel_id=1, source_target_pairs={{0,2},{1,3},{2,0},{3,1},{4,6},{5,7},{6,4},{7,5},{8,10},{9,11},{10,... | collective-permute-start | bytes 294920 | tf_op jit(solution)/shard_map/ppermute | solution.py:207
  4.0 10.4 %collective-permute-start.2 = (f32[3,32,256]{2,1,0:T(8,128)}, f32[3,32,256]{2,1,0:T(8,128)S(1)}, u32[]{:S(2)}, u32[]{:S(2)}) collective-permute-start(f32[3,32,256]{2,1,0:T(8,128)} %refs_0_.1), channel_id=1, source_target_pairs={{0,1},{1,0},{2,3},{3,2},{4,5},{5,4},{6,7},{7,6},{8,9},{9,8},{10,11... | collective-permute-start | bytes 294920 | tf_op jit(solution)/shard_map/ppermute | solution.py:207
  6.6 6.0 %collective-permute-start.5 = (f32[104,256]{1,0:T(8,128)S(1)}, f32[104,256]{1,0:T(8,128)S(1)}, u32[]{:S(2)}, u32[]{:S(2)}) collective-permute-start(f32[104,256]{1,0:T(8,128)S(1)} %pack.1.refs_0_), channel_id=1, source_target_pairs={{0,24},{4,28},{8,16},{12,20},{16,8},{20,12},{24,0},{28,4},{1,25},{... | collective-permute-start | bytes 319496 | tf_op jit(solution)/shard_map/ppermute | solution.py:207
  9.1 5.0 %collective-permute-start.4 = (f32[104,256]{1,0:T(8,128)S(1)}, f32[104,256]{1,0:T(8,128)S(1)}, u32[]{:S(2)}, u32[]{:S(2)}) collective-permute-start(f32[104,256]{1,0:T(8,128)S(1)} %pack.1.refs_0_), channel_id=1, source_target_pairs={{0,16},{4,20},{8,24},{12,28},{16,0},{20,4},{24,8},{28,12},{1,17},{... | collective-permute-start | bytes 319496 | tf_op jit(solution)/shard_map/ppermute | solution.py:207
  9.6 4.7 %collective-permute-start.3 = (f32[104,256]{1,0:T(8,128)S(1)}, f32[104,256]{1,0:T(8,128)S(1)}, u32[]{:S(2)}, u32[]{:S(2)}) collective-permute-start(f32[104,256]{1,0:T(8,128)S(1)} %pack.1.refs_0_), channel_id=1, source_target_pairs={{0,8},{4,12},{8,0},{12,4},{16,24},{20,28},{24,16},{28,20},{1,9},{5... | collective-permute-start | bytes 319496 | tf_op jit(solution)/shard_map/ppermute | solution.py:207
  10.1 4.3 %copy-start = (f32[3,32,256]{2,1,0:T(8,128)S(1)}, f32[3,32,256]{2,1,0:T(8,128)}, u32[]{:S(2)}) copy-start(f32[3,32,256]{2,1,0:T(8,128)} %refs_0_.1) | copy-start | bytes 294916
  10.1 5.4 %collective-permute-start.1 = (f32[3,32,256]{2,1,0:T(8,128)S(1)}, f32[3,32,256]{2,1,0:T(8,128)S(1)}, u32[]{:S(2)}, u32[]{:S(2)}) collective-permute-start(f32[3,32,256]{2,1,0:T(8,128)S(1)} %far_rows.1.refs_4_.refs_1_), channel_id=1, source_target_pairs={{0,1},{1,0},{2,3},{3,2},{4,5},{5,4},{6,7},{7,6},{8,9},{9,8},{10,11... | collective-permute-start | bytes 294920 | tf_op jit(solution)/shard_map/ppermute | solution.py:207
  14.3 1.8 %collective-permute-start.6 = (f32[4,104,256]{2,1,0:T(8,128)S(1)}, f32[4,104,256]{2,1,0:T(8,128)S(1)}, u32[]{:S(2)}, u32[]{:S(2)}) collective-permute-start(f32[4,104,256]{2,1,0:T(8,128)S(1)} %columns.1.refs_3_), channel_id=1, source_target_pairs={{0,4},{4,0},{8,12},{12,8},{16,20},{20,16},{24,28},{28,24},{1,5},{5... | collective-permute-start | bytes 1277960 | tf_op jit(solution)/shard_map/ppermute | solution.py:207
  17.4 5.7 %collective-permute-start.7 = (f32[32,128]{1,0:T(8,128)S(1)}, f32[32,128]{1,0:T(8,128)S(1)}, u32[]{:S(2)}, u32[]{:S(2)}) collective-permute-start(f32[32,128]{1,0:T(8,128)S(1)} %get-tuple-element.28), channel_id=1, source_target_pairs={{0,3},{1,2},{2,1},{3,0},{4,7},{5,6},{6,5},{7,4},{8,11},{9,10},{10,... | collective-permute-start | bytes 49160 | tf_op jit(solution)/shard_map/ppermute | solution.py:207
  19.4 4.6 %collective-permute-start.8 = (f32[32,128]{1,0:T(8,128)S(1)}, f32[32,128]{1,0:T(8,128)S(1)}, u32[]{:S(2)}, u32[]{:S(2)}) collective-permute-start(f32[32,128]{1,0:T(8,128)S(1)} %get-tuple-element.29), channel_id=1, source_target_pairs={{0,2},{1,3},{2,0},{3,1},{4,6},{5,7},{6,4},{7,5},{8,10},{9,11},{10,... | collective-permute-start | bytes 49160 | tf_op jit(solution)/shard_map/ppermute | solution.py:207
  19.4 4.6 %collective-permute-start.9 = (f32[32,128]{1,0:T(8,128)S(1)}, f32[32,128]{1,0:T(8,128)S(1)}, u32[]{:S(2)}, u32[]{:S(2)}) collective-permute-start(f32[32,128]{1,0:T(8,128)S(1)} %get-tuple-element.30), channel_id=1, source_target_pairs={{0,1},{1,0},{2,3},{3,2},{4,5},{5,4},{6,7},{7,6},{8,9},{9,8},{10,11... | collective-permute-start | bytes 49160 | tf_op jit(solution)/shard_map/ppermute | solution.py:207
where the time goes:
time: 24.9 us; the launch traced here: 24.7 us
  starting transfers between devices  14.2 us (57%)
  waiting for transfers between devices  5.89 us (24%)
  Pallas kernels  3.64 us (15%)
  other arithmetic  0.92 us (4%)
    ppermute x10, starting transfers between devices, exchange(): return lax.ppermute(x, axis, [(at, at ^ mask) for at in range(count)])  14.2 us
    ppermute x10, waiting for transfers between devices, exchange(): return lax.ppermute(x, axis, [(at, at ^ mask) for at in range(count)])  5.89 us
    pallas_call x7, Pallas kernels, call(): pl.pallas_call(kernel, out_shape=out_shape, in_specs=[VM] * len(ins), out...  3.64 us
    concatenate x1, other arithmetic, per_device(): jnp.concatenate([col_frames.reshape(comps * frames, atoms), jnp.pad(vecto...  0.92 us
  transfers between devices with their start and end apart: 10, of which 6 were waited for; matrix products, arithmetic and copies ran while one was open for 4% of the time, Pallas kernels for 7%

commit v1 on v0

--- a/solution.py
+++ b/solution.py
@@ -57,8 +57,8 @@
     coef_two = -2.0 * (
         s00 * s00 + s01 * s01 + s02 * s02 + s10 * s10 + s11 * s11 + s12 * s12 + s20 * s20 + s21 * s21 + s22 * s22
     )
-    coef_one = 8.0 * (s00 * s12 * s21 + s11 * s20 * s02 + s22 * s01 * s10) - 8.0 * (
-        s00 * s11 * s22 + s12 * s20 * s01 + s21 * s10 * s02
+    coef_one = -8.0 * (
+        s00 * (s11 * s22 - s12 * s21) + s01 * (s12 * s20 - s10 * s22) + s02 * (s10 * s21 - s11 * s20)
     )
     k00 = s00 + s11 + s22
     k11 = s00 - s11 - s22

time: 24.9 us -> 24.9 us (level)
  no operation moved by 1% of the time
where the time goes in v1:
time: 24.9 us; the launch traced here: 24.7 us
  starting transfers between devices  14.2 us (57%)
  waiting for transfers between devices  5.87 us (24%)
  Pallas kernels  3.67 us (15%)
  other arithmetic  0.92 us (4%)
    ppermute x10, starting transfers between devices, exchange(): return lax.ppermute(x, axis, [(at, at ^ mask) for at in range(count)])  14.2 us
    ppermute x10, waiting for transfers between devices, exchange(): return lax.ppermute(x, axis, [(at, at ^ mask) for at in range(count)])  5.87 us
    pallas_call x7, Pallas kernels, call(): pl.pallas_call(kernel, out_shape=out_shape, in_specs=[VM] * len(ins), out...  3.67 us
    concatenate x1, other arithmetic, per_device(): jnp.concatenate([col_frames.reshape(comps * frames, atoms), jnp.pad(vecto...  0.92 us
  transfers between devices with their start and end apart: 10, of which 6 were waited for; matrix products, arithmetic and copies ran while one was open for 4% of the time, Pallas kernels for 7%

profile of v1, /device:TPU:0, one launch (start us, length us, event | category | flops | bytes accessed | tf_op | source)
XLA Modules:
  0.0 24.7 jit_solution(1970082932757171391)
XLA Ops:
  0.0 4.0 %collective-permute-start = (f32[3,32,256]{2,1,0:T(8,128)}, f32[3,32,256]{2,1,0:T(8,128)S(1)}, u32[]{:S(2)}, u32[]{:S(2)}) collective-permute-start(f32[3,32,256]{2,1,0:T(8,128)} %refs_0_.1), channel_id=1, source_target_pairs={{0,2},{1,3},{2,0},{3,1},{4,6},{5,7},{6,4},{7,5},{8,10},{9,11},{10,... | collective-permute-start | bytes 294920 | tf_op jit(solution)/shard_map/ppermute | solution.py:207
  4.0 1.6 %collective-permute-start.2 = (f32[3,32,256]{2,1,0:T(8,128)}, f32[3,32,256]{2,1,0:T(8,128)S(1)}, u32[]{:S(2)}, u32[]{:S(2)}) collective-permute-start(f32[3,32,256]{2,1,0:T(8,128)} %refs_0_.1), channel_id=1, source_target_pairs={{0,1},{1,0},{2,3},{3,2},{4,5},{5,4},{6,7},{7,6},{8,9},{9,8},{10,11... | collective-permute-start | bytes 294920 | tf_op jit(solution)/shard_map/ppermute | solution.py:207
  5.6 0.9 %select_maximum_fusion.in_ref = f32[128,256]{1,0:T(8,128)S(1)} fusion(f32[32,64]{1,0:T(8,128)} %bitcast.4, f32[96,256]{1,0:T(8,128)} %bitcast.3), kind=kLoop, calls=%fused_computation | loop fusion | flops 98304 | bytes 237568 | tf_op jit(solution)/shard_map/concatenate | solution.py:234
  6.5 0.1 pack.1.refs_0_
  6.6 2.5 %collective-permute-start.5 = (f32[104,256]{1,0:T(8,128)S(1)}, f32[104,256]{1,0:T(8,128)S(1)}, u32[]{:S(2)}, u32[]{:S(2)}) collective-permute-start(f32[104,256]{1,0:T(8,128)S(1)} %pack.1.refs_0_), channel_id=1, source_target_pairs={{0,24},{4,28},{8,16},{12,20},{16,8},{20,12},{24,0},{28,4},{1,25},{... | collective-permute-start | bytes 319496 | tf_op jit(solution)/shard_map/ppermute | solution.py:207
  9.1 0.5 %collective-permute-start.4 = (f32[104,256]{1,0:T(8,128)S(1)}, f32[104,256]{1,0:T(8,128)S(1)}, u32[]{:S(2)}, u32[]{:S(2)}) collective-permute-start(f32[104,256]{1,0:T(8,128)S(1)} %pack.1.refs_0_), channel_id=1, source_target_pairs={{0,16},{4,20},{8,24},{12,28},{16,0},{20,4},{24,8},{28,12},{1,17},{... | collective-permute-start | bytes 319496 | tf_op jit(solution)/shard_map/ppermute | solution.py:207
  9.6 0.5 %collective-permute-start.3 = (f32[104,256]{1,0:T(8,128)S(1)}, f32[104,256]{1,0:T(8,128)S(1)}, u32[]{:S(2)}, u32[]{:S(2)}) collective-permute-start(f32[104,256]{1,0:T(8,128)S(1)} %pack.1.refs_0_), channel_id=1, source_target_pairs={{0,8},{4,12},{8,0},{12,4},{16,24},{20,28},{24,16},{28,20},{1,9},{5... | collective-permute-start | bytes 319496 | tf_op jit(solution)/shard_map/ppermute | solution.py:207
  10.1 0.0 collective-permute-done.in_ref
  10.1 0.0 copy-start
  10.1 0.5 %collective-permute-start.1 = (f32[3,32,256]{2,1,0:T(8,128)S(1)}, f32[3,32,256]{2,1,0:T(8,128)S(1)}, u32[]{:S(2)}, u32[]{:S(2)}) collective-permute-start(f32[3,32,256]{2,1,0:T(8,128)S(1)} %far_rows.1.refs_4_.refs_1_), channel_id=1, source_target_pairs={{0,1},{1,0},{2,3},{3,2},{4,5},{5,4},{6,7},{7,6},{8,9},{9,8},{10,11... | collective-permute-start | bytes 294920 | tf_op jit(solution)/shard_map/ppermute | solution.py:207
  10.7 2.0 %collective-permute-done.5.refs_3_ = f32[104,256]{1,0:T(8,128)S(1)} collective-permute-done((f32[104,256]{1,0:T(8,128)S(1)}, f32[104,256]{1,0:T(8,128)S(1)}, u32[]{:S(2)}, u32[]{:S(2)}) %collective-permute-start.5) | collective-permute-done | bytes 106528 | tf_op jit(solution)/shard_map/ppermute | solution.py:207
  12.7 1.4 %collective-permute-done.4.refs_2_ = f32[104,256]{1,0:T(8,128)S(1)} collective-permute-done((f32[104,256]{1,0:T(8,128)S(1)}, f32[104,256]{1,0:T(8,128)S(1)}, u32[]{:S(2)}, u32[]{:S(2)}) %collective-permute-start.4) | collective-permute-done | bytes 106528 | tf_op jit(solution)/shard_map/ppermute | solution.py:207
  14.1 0.2 collective-permute-done.3.refs_1_
  14.3 0.1 collective-permute-start.6
  14.4 0.0 collective-permute-done.2.refs_2_
  14.4 0.0 copy-done
  14.4 1.1 %early_tile.1 = (bf16[1,384,768]{2,1,0:T(8,128)(2,1)S(1)}, f32[1,128,128]{2,1,0:T(8,128)S(1)}, f32[1,128,128]{2,1,0:T(8,128)S(1)}, bf16[384,768]{1,0:T(8,128)(2,...) custom-call(f32[3,32,256]{2,1,0:T(8,128)S(1)} %copy-done, f32[3,32,256]{2,1,0:T(8,128)S(1)} %far_rows.1.refs_4_.refs_1_, ...), custom_call_target="tpu_custom_call" | custom-call | flops 226492416 | bytes 720896 | tf_op jit(solution)/shard_map/early_tile/pallas_call | solution.py:213
  15.5 0.0 collective-permute-done.1.row_ref
  15.5 0.5 %last_tile.1 = (bf16[1,384,768]{2,1,0:T(8,128)(2,1)S(1)}, f32[1,128,128]{2,1,0:T(8,128)S(1)}, f32[1,128,128]{2,1,0:T(8,128)S(1)}) custom-call(f32[3,32,256]{2,1,0:T(8,128)S(1)} %collective-permute-done.1.row_ref, bf16[384,768]{1,0:T(8,128)(2,1)S(1)} %get-tuple-element.18.side_ref, ...), custom_call_target="tpu_custom_call", output_to_operand_aliasing={{0}: (3, {}), {1}: (4, {}), {2}: (5, {})} | custom-call | flops 57982058496 | bytes 2592768 | tf_op jit(solution)/shard_map/last_tile/pallas_call | solution.py:213
  16.0 0.1 collective-permute-done.6.blocks_ref
  16.2 1.3 %second_tile.1 = (f32[32,128]{1,0:T(8,128)S(1)}, f32[32,128]{1,0:T(8,128)S(1)}, f32[32,128]{1,0:T(8,128)S(1)}, f32[32,128]{1,0:T(8,128)S(1)}) custom-call(bf16[1,384,768]{2,1,0:T(8,128)(2,1)S(1)} %get-tuple-element.23.rows_ref, f32[1,128,128]{2,1,0:T(8,128)S(1)} %get-tuple-element.24.row_norm_ref, f32[1,128,128]{2,1,0:T(8,128)S(1)} %get-tuple-element.25.tile_ref, ...), custom_call_target="tpu_custom_call" | custom-call | flops 226492416 | bytes 1933312 | tf_op jit(solution)/shard_map/second_tile/pallas_call | solution.py:213
  17.5 1.9 %collective-permute-start.7 = (f32[32,128]{1,0:T(8,128)S(1)}, f32[32,128]{1,0:T(8,128)S(1)}, u32[]{:S(2)}, u32[]{:S(2)}) collective-permute-start(f32[32,128]{1,0:T(8,128)S(1)} %get-tuple-element.28), channel_id=1, source_target_pairs={{0,3},{1,2},{2,1},{3,0},{4,7},{5,6},{6,5},{7,4},{8,11},{9,10},{10,... | collective-permute-start | bytes 49160 | tf_op jit(solution)/shard_map/ppermute | solution.py:207
  19.4 0.1 collective-permute-start.8
  19.5 2.5 %collective-permute-start.9 = (f32[32,128]{1,0:T(8,128)S(1)}, f32[32,128]{1,0:T(8,128)S(1)}, u32[]{:S(2)}, u32[]{:S(2)}) collective-permute-start(f32[32,128]{1,0:T(8,128)S(1)} %get-tuple-element.30), channel_id=1, source_target_pairs={{0,1},{1,0},{2,3},{3,2},{4,5},{5,4},{6,7},{7,6},{8,9},{9,8},{10,11... | collective-permute-start | bytes 49160 | tf_op jit(solution)/shard_map/ppermute | solution.py:207
  21.9 1.3 %collective-permute-done.7.refs_1_ = f32[32,128]{1,0:T(8,128)S(1)} collective-permute-done((f32[32,128]{1,0:T(8,128)S(1)}, f32[32,128]{1,0:T(8,128)S(1)}, u32[]{:S(2)}, u32[]{:S(2)}) %collective-permute-start.7) | collective-permute-done | bytes 16416 | tf_op jit(solution)/shard_map/ppermute | solution.py:207
  23.2 0.8 %collective-permute-done.8.refs_2_ = f32[32,128]{1,0:T(8,128)S(1)} collective-permute-done((f32[32,128]{1,0:T(8,128)S(1)}, f32[32,128]{1,0:T(8,128)S(1)}, u32[]{:S(2)}, u32[]{:S(2)}) %collective-permute-start.8) | collective-permute-done | bytes 16416 | tf_op jit(solution)/shard_map/ppermute | solution.py:207
  24.0 0.0 collective-permute-done.9.refs_3_
  24.0 0.7 %sum_divide.1 = f32[32,64]{1,0:T(8,128)} custom-call(f32[32,128]{1,0:T(8,128)S(1)} %get-tuple-element.27.refs_0_, f32[32,128]{1,0:T(8,128)S(1)} %collective-permute-done.7.refs_1_, f32[32,128]{1,0:T(8,128)S(1)} %collective-permute-done.8.refs_2_, f32[32,128]{1,0:T(8,128)S(1)} %collective-permute-done.9.refs_3_), custom_call_target="tpu_custom_call" | custom-call | bytes 65536 | tf_op jit(solution)/shard_map/sum_divide/pallas_call | solution.py:213
  (2 shorter events, 0.0 us)
Async XLA Ops:
  0.0 10.1 %collective-permute-start = (f32[3,32,256]{2,1,0:T(8,128)}, f32[3,32,256]{2,1,0:T(8,128)S(1)}, u32[]{:S(2)}, u32[]{:S(2)}) collective-permute-start(f32[3,32,256]{2,1,0:T(8,128)} %refs_0_.1), channel_id=1, source_target_pairs={{0,2},{1,3},{2,0},{3,1},{4,6},{5,7},{6,4},{7,5},{8,10},{9,11},{10,... | collective-permute-start | bytes 294920 | tf_op jit(solution)/shard_map/ppermute | solution.py:207
  4.0 10.4 %collective-permute-start.2 = (f32[3,32,256]{2,1,0:T(8,128)}, f32[3,32,256]{2,1,0:T(8,128)S(1)}, u32[]{:S(2)}, u32[]{:S(2)}) collective-permute-start(f32[3,32,256]{2,1,0:T(8,128)} %refs_0_.1), channel_id=1, source_target_pairs={{0,1},{1,0},{2,3},{3,2},{4,5},{5,4},{6,7},{7,6},{8,9},{9,8},{10,11... | collective-permute-start | bytes 294920 | tf_op jit(solution)/shard_map/ppermute | solution.py:207
  6.6 6.0 %collective-permute-start.5 = (f32[104,256]{1,0:T(8,128)S(1)}, f32[104,256]{1,0:T(8,128)S(1)}, u32[]{:S(2)}, u32[]{:S(2)}) collective-permute-start(f32[104,256]{1,0:T(8,128)S(1)} %pack.1.refs_0_), channel_id=1, source_target_pairs={{0,24},{4,28},{8,16},{12,20},{16,8},{20,12},{24,0},{28,4},{1,25},{... | collective-permute-start | bytes 319496 | tf_op jit(solution)/shard_map/ppermute | solution.py:207
  9.1 5.0 %collective-permute-start.4 = (f32[104,256]{1,0:T(8,128)S(1)}, f32[104,256]{1,0:T(8,128)S(1)}, u32[]{:S(2)}, u32[]{:S(2)}) collective-permute-start(f32[104,256]{1,0:T(8,128)S(1)} %pack.1.refs_0_), channel_id=1, source_target_pairs={{0,16},{4,20},{8,24},{12,28},{16,0},{20,4},{24,8},{28,12},{1,17},{... | collective-permute-start | bytes 319496 | tf_op jit(solution)/shard_map/ppermute | solution.py:207
  9.6 4.7 %collective-permute-start.3 = (f32[104,256]{1,0:T(8,128)S(1)}, f32[104,256]{1,0:T(8,128)S(1)}, u32[]{:S(2)}, u32[]{:S(2)}) collective-permute-start(f32[104,256]{1,0:T(8,128)S(1)} %pack.1.refs_0_), channel_id=1, source_target_pairs={{0,8},{4,12},{8,0},{12,4},{16,24},{20,28},{24,16},{28,20},{1,9},{5... | collective-permute-start | bytes 319496 | tf_op jit(solution)/shard_map/ppermute | solution.py:207
  10.1 4.3 %copy-start = (f32[3,32,256]{2,1,0:T(8,128)S(1)}, f32[3,32,256]{2,1,0:T(8,128)}, u32[]{:S(2)}) copy-start(f32[3,32,256]{2,1,0:T(8,128)} %refs_0_.1) | copy-start | bytes 294916
  10.1 5.4 %collective-permute-start.1 = (f32[3,32,256]{2,1,0:T(8,128)S(1)}, f32[3,32,256]{2,1,0:T(8,128)S(1)}, u32[]{:S(2)}, u32[]{:S(2)}) collective-permute-start(f32[3,32,256]{2,1,0:T(8,128)S(1)} %far_rows.1.refs_4_.refs_1_), channel_id=1, source_target_pairs={{0,1},{1,0},{2,3},{3,2},{4,5},{5,4},{6,7},{7,6},{8,9},{9,8},{10,11... | collective-permute-start | bytes 294920 | tf_op jit(solution)/shard_map/ppermute | solution.py:207
  14.3 1.8 %collective-permute-start.6 = (f32[4,104,256]{2,1,0:T(8,128)S(1)}, f32[4,104,256]{2,1,0:T(8,128)S(1)}, u32[]{:S(2)}, u32[]{:S(2)}) collective-permute-start(f32[4,104,256]{2,1,0:T(8,128)S(1)} %columns.1.refs_3_), channel_id=1, source_target_pairs={{0,4},{4,0},{8,12},{12,8},{16,20},{20,16},{24,28},{28,24},{1,5},{5... | collective-permute-start | bytes 1277960 | tf_op jit(solution)/shard_map/ppermute | solution.py:207
  17.5 5.8 %collective-permute-start.7 = (f32[32,128]{1,0:T(8,128)S(1)}, f32[32,128]{1,0:T(8,128)S(1)}, u32[]{:S(2)}, u32[]{:S(2)}) collective-permute-start(f32[32,128]{1,0:T(8,128)S(1)} %get-tuple-element.28), channel_id=1, source_target_pairs={{0,3},{1,2},{2,1},{3,0},{4,7},{5,6},{6,5},{7,4},{8,11},{9,10},{10,... | collective-permute-start | bytes 49160 | tf_op jit(solution)/shard_map/ppermute | solution.py:207
  19.4 4.6 %collective-permute-start.8 = (f32[32,128]{1,0:T(8,128)S(1)}, f32[32,128]{1,0:T(8,128)S(1)}, u32[]{:S(2)}, u32[]{:S(2)}) collective-permute-start(f32[32,128]{1,0:T(8,128)S(1)} %get-tuple-element.29), channel_id=1, source_target_pairs={{0,2},{1,3},{2,0},{3,1},{4,6},{5,7},{6,4},{7,5},{8,10},{9,11},{10,... | collective-permute-start | bytes 49160 | tf_op jit(solution)/shard_map/ppermute | solution.py:207
  19.5 4.6 %collective-permute-start.9 = (f32[32,128]{1,0:T(8,128)S(1)}, f32[32,128]{1,0:T(8,128)S(1)}, u32[]{:S(2)}, u32[]{:S(2)}) collective-permute-start(f32[32,128]{1,0:T(8,128)S(1)} %get-tuple-element.30), channel_id=1, source_target_pairs={{0,1},{1,0},{2,3},{3,2},{4,5},{5,4},{6,7},{7,6},{8,9},{9,8},{10,11... | collective-permute-start | bytes 49160 | tf_op jit(solution)/shard_map/ppermute | solution.py:207
